TPU v7x, 32 devices: a whole 2x2x4 slice. The times are simulated.
32 devices in a mesh: blk: 4 (over y, core), bal: 8 (over z, x).
Axes of the slice: x: 2, y: 2, z: 4, core: 2. Of those that a mesh axis runs over, the one named last changes fastest.
Arguments:
- features: bfloat16 [32768, 512], P('blk', 'bal'), may hold values from -6 to 6
- tile_values: bfloat16 [4, 4, 32, 128, 128], P('blk'), may hold values from 0.049804688 to 1
- tile_rows: int32 [4, 4, 32], P('blk'), may hold values from 0 to 63
- tile_cols: int32 [4, 4, 32], P('blk'), may hold values from 0 to 63
- tile_counts: int32 [4, 4], P('blk'), may hold values from 8 to 32, as said below
- w_self: bfloat16 [512, 512], replicated, may hold values from -0.25 to 0.25
- w_neigh: bfloat16 [512, 512], replicated, may hold values from -5 to 5
- bias: float32 [512], replicated, may hold values from -3 to 3
- part_map: int32 [4, 64], P('blk'), may hold values from 0 to 7, as said below
Outputs:
- next_rows: bfloat16 [4, 8, 2048, 512], P('blk', 'bal')
Inputs may be any that keep to these rules, and one draw needn't show every extreme that they name: `tile_counts`: live slots of one pair of vertex blocks; the most, 32, is reached by some pair in every draw. `part_map`: within one block of vertex rows at most 16 tiles go to any one value, and exactly 16 to some value.
All inputs are finite; a program needn't handle non-finite values.
Results may differ from a plain program's by a relative error of at most 0.0036.
Values may be sent and summed in bfloat16 or wider, within the bound.
A program may use at most 128 MiB of HBM per device.

v0:
```python
import functools
import jax
import jax.numpy as jnp
from jax import lax
from jax.experimental import pallas as pl
from jax.experimental.pallas import tpu as pltpu
from jax.sharding import PartitionSpec as P

TILE = 128
HALF = 64
MESH = pl.DeviceIdType.MESH


def from_behind(block, axis, distance):
    devices = range(lax.axis_size(axis))
    route = [((i - distance) % len(devices), i) for i in devices]
    return lax.ppermute(block, axis, route)


def advance(block, steps_by):
    return from_behind(block, "blk", steps_by)


def on_device(
    features, tile_values, tile_rows, tile_cols, tile_counts, w_self, w_neigh, bias, part_map
):
    n_blk = lax.axis_size("blk")
    n_bal = lax.axis_size("bal")
    here = lax.axis_index("blk")
    column = lax.axis_index("bal")
    width = features.shape[1]
    tiles_per = part_map.shape[1]
    values = tile_values[0]
    rows_idx = tile_rows[0]
    cols_idx = tile_cols[0]
    counts = tile_counts[0]
    slots = values.shape[1]
    live = jnp.arange(slots)[None, :] < counts[:, None]
    row_hot = (
        (rows_idx[:, :, None] == jnp.arange(tiles_per)[None, None, :]) & live[:, :, None]
    ).astype(jnp.float32)
    row_mass = jnp.einsum(
        "csij,j->csi", values, jnp.ones((TILE,), jnp.bfloat16), preferred_element_type=jnp.float32
    )
    degree = 1.0 + jnp.einsum("cst,csi->ti", row_hot, row_mass, precision=lax.Precision.HIGHEST)

    def absorb(total, block, source):
        tiles = block.reshape(tiles_per, TILE, width)
        vals = lax.dynamic_index_in_dim(values, source, 0, keepdims=False)
        picks = lax.dynamic_index_in_dim(cols_idx, source, 0, keepdims=False)
        targets = lax.dynamic_index_in_dim(rows_idx, source, 0, keepdims=False)
        alive = lax.dynamic_index_in_dim(live, source, 0, keepdims=False)
        gathered = jnp.take(tiles, picks, axis=0)
        prod = jnp.einsum("sij,sjf->sif", vals, gathered, preferred_element_type=jnp.float32)
        masked = jnp.where(alive[:, None, None], prod, 0.0)
        return total.at[targets].add(masked)

    empty = jnp.zeros((tiles_per, TILE, width), jnp.float32)

    def step_one(index, carry):
        total, block = carry
        total = absorb(total, block, (here - index) % n_blk)
        block = advance(block, 1)
        return (total, block)

    total, block = lax.fori_loop(0, n_blk - 1, step_one, (empty, features))
    total = absorb(total, block, (here - (n_blk - 1)) % n_blk)
    mean_agg = (total / degree[:, :, None]).astype(jnp.bfloat16).reshape(tiles_per * TILE, width)
    capacity = 2 * tiles_per // n_bal
    mapping = part_map[0]
    dest_hot = (mapping[:, None] == jnp.arange(n_bal)[None, :]).astype(jnp.int32)
    ranks = jnp.cumsum(dest_hot, axis=0) - dest_hot
    place = mapping * capacity + jnp.sum(ranks * dest_hot, axis=1)
    select = (jnp.arange(n_bal * capacity)[:, None] == place[None, :]).astype(jnp.bfloat16)
    col_start = column * width
    zeros_out = jnp.zeros((tiles_per * TILE, width), jnp.float32)
    carry = zeros_out
    mean_piece = lax.all_gather(mean_agg, "bal", axis=1, tiled=True)
    feat_piece = lax.all_gather(features, "bal", axis=1, tiled=True)
    count = mean_piece.shape[1]
    neigh_part = lax.dynamic_slice(w_neigh, (0, col_start), (count, width))
    self_part = lax.dynamic_slice(w_self, (0, col_start), (count, width))
    carry = jnp.dot(mean_piece, neigh_part, preferred_element_type=jnp.float32)
    pre = carry + jnp.dot(feat_piece, self_part, preferred_element_type=jnp.float32)
    pre = pre + lax.dynamic_slice_in_dim(bias, col_start, width)
    hidden = jnp.maximum(pre, 0.0).astype(jnp.bfloat16)
    tiles = hidden.reshape(tiles_per, TILE, width)
    placed = jnp.einsum("kt,tif->kif", select, tiles, preferred_element_type=jnp.float32)
    result = lax.all_to_all(
        placed.astype(jnp.bfloat16).reshape(n_bal, capacity * TILE, width),
        "bal",
        split_axis=0,
        concat_axis=2,
        tiled=True,
    )
    return result[None]


def tables(pm_ref, rows_ref, cols_ref, counts_ref, table, slots, cap):
    n_src = rows_ref.shape[0]
    table[...] = jnp.zeros(table.shape, jnp.int32)
    square = (TILE, TILE)
    lane = lax.broadcasted_iota(jnp.int32, square, 1)
    sub = lax.broadcasted_iota(jnp.int32, square, 0)

    def spread(row):
        return jnp.broadcast_to(row, square)

    def total(x):
        return jnp.sum(x, axis=0, keepdims=True)

    def flat(ref):
        return jnp.concatenate([ref[c : c + 1, :] for c in range(n_src)], axis=1)

    pm = pm_ref[...]
    pm = jnp.concatenate([pm, jnp.full((1, TILE - pm.shape[1]), 999, jnp.int32)], axis=1)
    pm_r = spread(pm)
    pm_c = pm_r.T
    earlier = jnp.where((pm_c == pm_r) & (sub < lane), 1, 0)
    place_c = spread(pm * cap + total(earlier)).T
    table[0:1, :] = total(jnp.where(place_c == lane, sub, 0))
    table[8:9, :] = total(jnp.where(pm_c == lane // cap, 1, 0))

    lane_row = lax.broadcasted_iota(jnp.int32, (1, TILE), 1)
    alive = jnp.zeros((1, TILE), jnp.int32)
    for c in range(n_src):
        alive = jnp.where(lane_row // slots == c, counts_ref[0, c], alive)
    rows_r = spread(flat(rows_ref))
    goes = total(jnp.where(rows_r == sub, place_c, 0))
    goes = jnp.where(lane_row % slots < alive, goes, 4096)
    goes_r = spread(goes)
    goes_c = goes_r.T
    rank_c = spread(total(jnp.where(goes_c * TILE + sub < goes_r * TILE + lane, 1, 0))).T
    pick = rank_c == lane
    source = (lane_row // slots) * HALF + flat(cols_ref)
    source_c = spread(source).T
    table[1:2, :] = total(jnp.where(pick, sub, 0))
    table[2:3, :] = total(jnp.where(pick, source_c, 0))
    mine = total(jnp.where(pick, goes_c, 0))
    before = total(jnp.where(rank_c + 1 == lane, goes_c, 0))
    table[3:4, :] = jnp.where((mine == before) & (lane_row % HALF != 0), 1, 0)
    upto = total(jnp.where(goes_c <= lane, 1, 0))
    below = total(jnp.where(goes_c < lane, 1, 0))
    left_end = jnp.minimum(upto, HALF)
    right_from = jnp.maximum(below, HALF)
    table[4:5, :] = jnp.maximum(left_end - 1, 0)
    table[5:6, :] = jnp.where(below < left_end, 1, 0)
    table[6:7, :] = jnp.maximum(upto - 1 - HALF, 0)
    table[7:8, :] = jnp.where(right_from < upto, 1, 0)


def layer_kernel(
    cap, slots, n_y, n_m, n_q, swap,
    feat, vals_hbm, rows_ref, cols_ref, counts_ref, ws_hbm, wn_hbm, bias_ref, pm_ref,
    out_v,
    vals, own, mirror, blocks, mirrors, sums, more, f_in, f_out, f_recv, m_in, m_out, m_recv, pre,
    ws_ref, wn_ref, table_v, table,
    vals_sem, ws_sem, wn_sem, table_sem, mir_sem,
    swap_send, swap_recv, sib_send, sib_recv, y_send, y_recv, fwd_send, fwd_recv,
    msib_send, msib_recv, my_send, my_recv, mfwd_send, mfwd_recv,
    fs_sem, fr_sem, fms_sem, fmr_sem, ms_sem, mr_sem, mms_sem, mmr_sem,
):
    here = lax.axis_index("blk")
    me = lax.axis_index("bal")
    tiles, width, _ = own.shape
    wide = width + swap
    stay = width - swap
    n_bal = f_recv.shape[1] // width
    half = n_bal // 2
    base = me // half * half
    partner = (me + half) % n_bal
    sibling = here + 1 - 2 * (here % 2)
    across = (here + 2) % 4
    far = (sibling + 2) % 4
    y_tiles = tiles // n_y
    m_tiles = tiles // n_m
    q_tiles = cap // n_q
    own_rows = pl.ds(pl.multiple_of(me * width, width), width)
    mirror_rows = pl.ds(pl.multiple_of(partner * width + stay, 16), swap)

    def near(o):
        return base + (me + o) % half

    def other(o):
        return (base + half) % n_bal + (me + o) % half

    def each(first, last, body):
        def step(i, carry):
            body(i)
            return carry

        lax.fori_loop(first, last, step, 0)

    def remote(src, dst, send, recv, axis, peer):
        return pltpu.make_async_remote_copy(
            src, dst, send, recv, device_id={axis: peer}, device_id_type=MESH
        )

    load_vals = pltpu.make_async_copy(vals_hbm, vals, vals_sem)
    load_vals.start()
    load_ws = pltpu.make_async_copy(ws_hbm, ws_ref, ws_sem)
    load_ws.start()
    load_wn = pltpu.make_async_copy(wn_hbm, wn_ref, wn_sem)
    load_wn.start()

    barrier = pltpu.get_barrier_semaphore()
    for peer in (sibling, across):
        pl.semaphore_signal(barrier, inc=1, device_id={"blk": peer}, device_id_type=MESH)
    each(
        1, n_bal,
        lambda o: pl.semaphore_signal(
            barrier, inc=1, device_id={"bal": (me + o) % n_bal}, device_id_type=MESH
        ),
    )

    def pack(t):
        x = feat[:, pl.ds(pl.multiple_of(t * TILE, TILE), TILE)]
        own[t] = x
        blocks[here * tiles + t] = x

    each(0, tiles, pack)
    pl.semaphore_wait(barrier, n_bal + 1)

    def swap_copy(i):
        span = pl.ds(i * m_tiles, m_tiles)
        return remote(
            own.at[span, pl.ds(stay, swap)], mirror.at[span],
            swap_send.at[i], swap_recv.at[i], "bal", partner,
        )

    def y_copy(i, whose):
        return remote(
            own.at[pl.ds(i * y_tiles, y_tiles)],
            blocks.at[pl.ds(whose * tiles + i * y_tiles, y_tiles)],
            y_send.at[i], y_recv.at[i], "blk", across,
        )

    def fwd_copy(i, whose):
        span = pl.ds(whose * tiles + i * y_tiles, y_tiles)
        part = blocks.at[span]
        return remote(part, part, fwd_send.at[i], fwd_recv.at[i], "blk", sibling)

    def sib_copy(whose):
        return remote(
            own, blocks.at[pl.ds(whose * tiles, tiles)],
            sib_send, sib_recv, "blk", sibling,
        )

    def my_copy(i, whose):
        return remote(
            mirror.at[pl.ds(i * m_tiles, m_tiles)],
            mirrors.at[pl.ds(whose * tiles + i * m_tiles, m_tiles)],
            my_send.at[i], my_recv.at[i], "blk", across,
        )

    def msib_copy(i, whose):
        return remote(
            mirror.at[pl.ds(i * m_tiles, m_tiles)],
            mirrors.at[pl.ds(whose * tiles + i * m_tiles, m_tiles)],
            msib_send.at[i], msib_recv.at[i], "blk", sibling,
        )

    def mfwd_copy(i, whose):
        span = pl.ds(whose * tiles + i * m_tiles, m_tiles)
        part = mirrors.at[span]
        return remote(part, part, mfwd_send.at[i], mfwd_recv.at[i], "blk", sibling)

    def f_near(o, whose):
        rows = pl.ds(pl.multiple_of(whose * width, width), width)
        return remote(
            f_in.at[o, :, pl.ds(0, width)], f_recv.at[:, rows],
            fs_sem.at[o], fr_sem.at[whose], "bal", near(o),
        )

    def f_near_mirror(o, whose):
        rows = pl.ds(pl.multiple_of((whose + half) % n_bal * width + stay, 16), swap)
        return remote(
            f_in.at[o, :, pl.ds(width, swap)], f_recv.at[:, rows],
            fms_sem.at[o], fmr_sem.at[whose], "bal", near(o),
        )

    def f_other(o, whose):
        rows = pl.ds(pl.multiple_of(whose * width, width), stay)
        return remote(
            f_out.at[o], f_recv.at[:, rows],
            fs_sem.at[half + o], fr_sem.at[whose], "bal", other(o),
        )

    def m_near(q, o, whose):
        span = pl.ds(q * q_tiles, q_tiles)
        rows = pl.ds(pl.multiple_of(whose * width, width), width)
        return remote(
            m_in.at[o, span, pl.ds(0, width)], m_recv.at[span, rows],
            ms_sem.at[q, o], mr_sem.at[q, whose], "bal", near(o),
        )

    def m_near_mirror(q, o, whose):
        span = pl.ds(q * q_tiles, q_tiles)
        rows = pl.ds(pl.multiple_of((whose + half) % n_bal * width + stay, 16), swap)
        return remote(
            m_in.at[o, span, pl.ds(width, swap)], m_recv.at[span, rows],
            mms_sem.at[q, o], mmr_sem.at[q, whose], "bal", near(o),
        )

    def m_other(q, o, whose):
        span = pl.ds(q * q_tiles, q_tiles)
        rows = pl.ds(pl.multiple_of(whose * width, width), stay)
        return remote(
            m_out.at[o, span], m_recv.at[span, rows],
            ms_sem.at[q, half + o], mr_sem.at[q, whose], "bal", other(o),
        )

    each(0, n_m, lambda i: swap_copy(i).start())
    each(0, n_y, lambda i: y_copy(i, here).start())
    sib_copy(here).start()

    tables(pm_ref, rows_ref, cols_ref, counts_ref, table_v, slots, cap)
    load_table = pltpu.make_async_copy(table_v, table, table_sem)
    load_table.start()
    load_table.wait()

    def send_f_near(o):
        def gather(k):
            f_in[o, k, :width, :] = own[table[0, near(o) * cap + k]]

        each(0, cap, gather)
        f_near(o, me).start()

    def fill_f_other(o):
        def gather(k):
            f_out[o, k] = own[table[0, other(o) * cap + k]][:stay]

        each(0, cap, gather)

    def keep_f(k):
        f_recv[k, own_rows, :] = own[table[0, me * cap + k]]

    each(1, half, send_f_near)
    if stay:
        each(0, half, fill_f_other)
    each(0, cap, keep_f)
    load_vals.wait()

    def pass_on(i):
        y_copy(i, across).wait_recv()
        fwd_copy(i, across).start()

    def take_mirror(i):
        swap_copy(i).wait_recv()
        my_copy(i, here).start()
        msib_copy(i, here).start()

    each(0, n_y, pass_on)
    each(0, n_m, take_mirror)
    if stay:
        each(0, half, lambda o: f_other(o, me).start())
    keep_mirror = pltpu.make_async_copy(
        mirror, mirrors.at[pl.ds(here * tiles, tiles)], mir_sem
    )
    keep_mirror.start()

    def send_f_mirror(o):
        def gather(k):
            f_in[o, k, width:, :] = mirror[table[0, near(o) * cap + k]]

        each(0, cap, gather)
        f_near_mirror(o, me).start()

    def keep_f_mirror(k):
        f_recv[k, mirror_rows, :] = mirror[table[0, me * cap + k]]

    each(1, half, send_f_mirror)
    each(0, cap, keep_f_mirror)

    sib_copy(sibling).wait_recv()
    each(0, n_y, lambda i: fwd_copy(i, far).wait_recv())

    in_top = lax.broadcasted_iota(jnp.int32, (16, 2 * TILE), 0) < 8
    in_left = lax.broadcasted_iota(jnp.int32, (16, 2 * TILE), 1) < TILE
    ones = jnp.where(in_top == in_left, 1.0, 0.0).astype(jnp.bfloat16)
    deg_left = lax.broadcasted_iota(jnp.int32, (16, TILE), 0) < 8

    def products(j, held, count, extra):
        zeros = jnp.zeros((count, TILE), jnp.bfloat16)
        a = jnp.concatenate([vals[table[1, j]], vals[table[1, j + HALF]]], axis=1)
        x = jnp.concatenate([held[table[2, j]], zeros], axis=1)
        y = jnp.concatenate([zeros, held[table[2, j + HALF]]], axis=1)
        lhs = jnp.concatenate([x, y] + extra, axis=0)
        return lax.dot_general(
            lhs, a, (((1,), (1,)), ((), ())), preferred_element_type=jnp.float32
        )

    def absorb(j, carry):
        left, right, deg = carry
        prod = products(j, blocks, width, [ones])
        keep_left, keep_right = table[3, j], table[3, j + HALF]
        left = jnp.where(keep_left > 0, left, 0.0) + prod[:width]
        right = jnp.where(keep_right > 0, right, 0.0) + prod[width : 2 * width]
        deg = jnp.where(jnp.where(deg_left, keep_left, keep_right) > 0, deg, 0.0)
        deg = deg + prod[2 * width :]
        sums[j, :width, :] = left
        sums[j, width : 2 * width, :] = right
        sums[j, 2 * width :, :] = deg
        return left, right, deg

    def absorb_mirror(j, carry):
        left, right = carry
        prod = products(j, mirrors, swap, [])
        left = jnp.where(table[3, j] > 0, left, 0.0) + prod[:swap]
        right = jnp.where(table[3, j + HALF] > 0, right, 0.0) + prod[swap:]
        more[j, :swap, :] = left
        more[j, swap:, :] = right
        return left, right

    empty = jnp.zeros((width, TILE), jnp.float32)
    lax.fori_loop(
        0, HALF, absorb, (empty, empty, jnp.zeros((16, TILE), jnp.float32)), unroll=2
    )

    def inverse_degree(p):
        left, right = sums.at[table[4, p]], sums.at[table[6, p]]
        degree = (
            1.0
            + jnp.where(table[5, p] > 0, left[2 * width : 2 * width + 8, :], 0.0)
            + jnp.where(table[7, p] > 0, right[2 * width + 8 :, :], 0.0)
        )
        return (1.0 / degree)[:1]

    def mean_piece(p, inverse, where, count, right_row):
        left, right = where.at[table[4, p]], where.at[table[6, p]]
        agg = jnp.where(table[5, p] > 0, left[:count, :], 0.0) + jnp.where(
            table[7, p] > 0, right[right_row : right_row + count, :], 0.0
        )
        return (agg * inverse).astype(jnp.bfloat16)

    def send_m_other(q):
        def to_other(o):
            def fill(k):
                p = other(o) * cap + q * q_tiles + k
                m_out[o, q * q_tiles + k] = mean_piece(p, inverse_degree(p), sums, stay, width)

            each(0, q_tiles, fill)
            m_other(q, o, me).start()

        each(0, half, to_other)

    def pass_mirror_on(i):
        my_copy(i, across).wait_recv()
        mfwd_copy(i, across).start()

    if stay:
        each(0, n_q, send_m_other)
    each(0, n_m, pass_mirror_on)
    each(0, n_m, lambda i: msib_copy(i, sibling).wait_recv())
    each(0, n_m, lambda i: mfwd_copy(i, far).wait_recv())
    keep_mirror.wait()
    lax.fori_loop(0, HALF, absorb_mirror, (empty[:swap], empty[:swap]), unroll=2)

    def send_m(q):
        def to_near(o):
            def fill(k):
                p = near(o) * cap + q * q_tiles + k
                inverse = inverse_degree(p)
                at = q * q_tiles + k
                m_in[o, at, :width, :] = mean_piece(p, inverse, sums, width, width)
                m_in[o, at, width:, :] = mean_piece(p, inverse, more, swap, swap)

            each(0, q_tiles, fill)
            m_near(q, o, me).start()
            m_near_mirror(q, o, me).start()

        each(1, half, to_near)

    each(0, n_q, send_m)

    def keep_m(k):
        p = me * cap + k
        inverse = inverse_degree(p)
        m_recv[k, own_rows, :] = mean_piece(p, inverse, sums, width, width)
        m_recv[k, mirror_rows, :] = mean_piece(p, inverse, more, swap, swap)

    each(0, cap, keep_m)
    load_ws.wait()
    load_wn.wait()

    def wait_f_near(o):
        f_near(o, near(o)).wait_recv()
        f_near_mirror(o, near(o)).wait_recv()

    each(1, half, wait_f_near)
    if stay:
        each(0, half, lambda o: f_other(o, other(o)).wait_recv())

    rows = q_tiles * TILE

    def times(recv, q, weight):
        x = jnp.concatenate([recv[q * q_tiles + k] for k in range(q_tiles)], axis=1)
        return lax.dot_general(
            x, weight[...], (((0,), (0,)), ((), ())), preferred_element_type=jnp.float32
        )

    def chunk(q):
        return pl.ds(pl.multiple_of(q * rows, rows), rows)

    def self_part(q):
        pre[chunk(q), :] = times(f_recv, q, ws_ref) + bias_ref[...]

    each(0, n_q, self_part)
    live = table[8, me * cap]

    def finish(q):
        def wait_near(o):
            m_near(q, o, near(o)).wait_recv()
            m_near_mirror(q, o, near(o)).wait_recv()

        each(1, half, wait_near)
        if stay:
            each(0, half, lambda o: m_other(q, o, other(o)).wait_recv())
        hidden = jnp.maximum(pre[chunk(q), :] + times(m_recv, q, wn_ref), 0.0)
        row = q * rows + lax.broadcasted_iota(jnp.int32, (rows, 1), 0)
        out_v[0, 0, chunk(q), :] = jnp.where(row < live * TILE, hidden, 0.0).astype(jnp.bfloat16)

    each(0, n_q, finish)

    def settle_near(o):
        f_near(o, me).wait_send()
        f_near_mirror(o, me).wait_send()

        def one(q):
            m_near(q, o, me).wait_send()
            m_near_mirror(q, o, me).wait_send()

        each(0, n_q, one)

    def settle_other(o):
        f_other(o, me).wait_send()
        each(0, n_q, lambda q: m_other(q, o, me).wait_send())

    def settle_y(i):
        y_copy(i, here).wait_send()
        fwd_copy(i, across).wait_send()

    def settle_mirror(i):
        swap_copy(i).wait_send()
        my_copy(i, here).wait_send()
        msib_copy(i, here).wait_send()
        mfwd_copy(i, across).wait_send()

    each(1, half, settle_near)
    if stay:
        each(0, half, settle_other)
    each(0, n_y, settle_y)
    each(0, n_m, settle_mirror)
    sib_copy(here).wait_send()


def layer(
    features, tile_values, tile_rows, tile_cols, tile_counts, w_self, w_neigh, bias, part_map
):
    n_blk = lax.axis_size("blk")
    n_bal = lax.axis_size("bal")
    slots = tile_rows.shape[2]
    tiles = part_map.shape[1]
    cap = 2 * tiles // n_bal
    width = features.shape[1]
    total = w_self.shape[0]
    fits = (
        n_blk == 4 and n_blk * slots == TILE and tiles == HALF and width == HALF
        and n_bal * cap == TILE
    )
    if not fits:
        return on_device(
            features, tile_values, tile_rows, tile_cols, tile_counts, w_self, w_neigh, bias,
            part_map,
        )
    n_y, n_m, n_q = 4, 2, 4
    swap = width // 2
    wide, stay, half = width + swap, width - swap, n_bal // 2
    bf16, f32 = jnp.bfloat16, jnp.float32
    vmem = pl.BlockSpec(memory_space=pltpu.VMEM)
    smem = pl.BlockSpec(memory_space=pltpu.SMEM)
    hbm = pl.BlockSpec(memory_space=pl.ANY)
    dma = pltpu.SemaphoreType.DMA
    return pl.pallas_call(
        functools.partial(layer_kernel, cap, slots, n_y, n_m, n_q, swap),
        out_shape=pltpu.VMEM((1, 1, cap * TILE, total), bf16),
        in_specs=[vmem, hbm, vmem, vmem, smem, hbm, hbm, vmem, vmem],
        out_specs=vmem,
        scratch_shapes=[
            pltpu.VMEM((n_blk * slots, TILE, TILE), bf16),
            pltpu.VMEM((tiles, width, TILE), bf16),
            pltpu.VMEM((tiles, swap, TILE), bf16),
            pltpu.VMEM((n_blk * tiles, width, TILE), bf16),
            pltpu.VMEM((n_blk * tiles, swap, TILE), bf16),
            pltpu.VMEM((HALF, 2 * width + 16, TILE), f32),
            pltpu.VMEM((HALF, 2 * swap, TILE), f32),
            pltpu.VMEM((half, cap, wide, TILE), bf16),
            pltpu.VMEM((half, cap, max(stay, 16), TILE), bf16),
            pltpu.VMEM((cap, total, TILE), bf16),
            pltpu.VMEM((half, cap, wide, TILE), bf16),
            pltpu.VMEM((half, cap, max(stay, 16), TILE), bf16),
            pltpu.VMEM((cap, total, TILE), bf16),
            pltpu.VMEM((cap * TILE, total), f32),
            pltpu.VMEM((total, total), bf16),
            pltpu.VMEM((total, total), bf16),
            pltpu.VMEM((16, TILE), jnp.int32),
            pltpu.SMEM((16, TILE), jnp.int32),
            dma, dma, dma, dma, dma,
            dma((n_m,)), dma((n_m,)), dma, dma, dma((n_y,)), dma((n_y,)), dma((n_y,)), dma((n_y,)),
            dma((n_m,)), dma((n_m,)), dma((n_m,)), dma((n_m,)), dma((n_m,)), dma((n_m,)),
            dma((n_bal,)), dma((n_bal,)), dma((half,)), dma((n_bal,)),
            dma((n_q, n_bal)), dma((n_q, n_bal)), dma((n_q, half)), dma((n_q, n_bal)),
        ],
        compiler_params=pltpu.CompilerParams(
            collective_id=0, has_side_effects=True, vmem_limit_bytes=56 * 2**20
        ),
        cost_estimate=pl.CostEstimate(
            flops=4 * cap * TILE * total * total, bytes_accessed=12 * 2**20, transcendentals=0
        ),
    )(
        features.T,
        tile_values.reshape(n_blk * slots, TILE, TILE),
        tile_rows[0],
        tile_cols[0],
        tile_counts,
        w_self,
        w_neigh,
        bias.reshape(1, total),
        part_map,
    )


def solution(mesh):
    placed = (
        P("blk", "bal"),
        P("blk", None, None, None, None),
        P("blk", None, None),
        P("blk", None, None),
        P("blk", None),
        P(),
        P(),
        P(),
        P("blk", None),
    )
    return jax.shard_map(
        layer,
        mesh=mesh,
        in_specs=placed,
        out_specs=P("blk", "bal", None, None),
        check_vma=False,
    )
```

profile of v0, /device:TPU:0, one launch (start us, length us, event | category | flops | bytes accessed | tf_op | source)
XLA Modules:
  0.0 82.2 jit_solution(5095793908950014204)
XLA Ops:
  0.0 80.8 %shard_map.91 = bf16[1,1,2048,512]{3,2,1,0:T(8,128)(2,1)S(1)} custom-call(bf16[64,8192]{1,0:T(8,128)(2,1)} %bitcast.6, bf16[128,128,128]{2,1,0:T(8,128)(2,1)} %bitcast.5, s32[4,32]{1,0:T(4,128)} %bitcast.7, s32[4,32]{1,0:T(4,128)} %bitcast.8, s32[1,4]{1,0:T(1,128)} %counts_ref.1, bf16[512,512]{1,0:T(8,128)(2,1)} %ws_hbm.1, bf16[512,512]{1,0:T(8,128)(2,1)} %wn_hbm.1, ...), custom_call_target="tpu_custom_call" | custom-call | flops 2147483648 | bytes 12582912 | tf_op jit(solution)/shard_map/pallas_call | solution.py:584
  80.9 1.3 %copy.11 = bf16[1,1,2048,512]{3,2,1,0:T(8,128)(2,1)} copy(bf16[1,1,2048,512]{3,2,1,0:T(8,128)(2,1)S(1)} %shard_map.91) | data formatting | bytes 4194304
where the time goes:
time: 83.3 us; the launch traced here: 82.2 us
  Pallas kernels  80.8 us (97%)
  local copies, waits for them, and re-layouts  1.32 us (2%)
    pallas_call x1, Pallas kernels, layer(): pl.pallas_call(functools.partial(layer_kernel, cap, slots, n_y, n_m, n_q,...  80.8 us

commit v1 on v0

--- a/solution.py
+++ b/solution.py
@@ -351,9 +351,10 @@
         msib_copy(i, here).start()
 
     each(0, n_y, pass_on)
-    each(0, n_m, take_mirror)
+    each(0, n_m - 1, take_mirror)
     if stay:
         each(0, half, lambda o: f_other(o, me).start())
+    each(n_m - 1, n_m, take_mirror)
     keep_mirror = pltpu.make_async_copy(
         mirror, mirrors.at[pl.ds(here * tiles, tiles)], mir_sem
     )
@@ -444,6 +445,19 @@
 
         each(0, half, to_other)
 
+    def send_m_near(q):
+        def to_near(o):
+            def fill(k):
+                p = near(o) * cap + q * q_tiles + k
+                m_in[o, q * q_tiles + k, :width, :] = mean_piece(
+                    p, inverse_degree(p), sums, width, width
+                )
+
+            each(0, q_tiles, fill)
+            m_near(q, o, me).start()
+
+        each(1, half, to_near)
+
     def pass_mirror_on(i):
         my_copy(i, across).wait_recv()
         mfwd_copy(i, across).start()
@@ -451,27 +465,26 @@
     if stay:
         each(0, n_q, send_m_other)
     each(0, n_m, pass_mirror_on)
+    each(0, n_q, send_m_near)
     each(0, n_m, lambda i: msib_copy(i, sibling).wait_recv())
     each(0, n_m, lambda i: mfwd_copy(i, far).wait_recv())
     keep_mirror.wait()
     lax.fori_loop(0, HALF, absorb_mirror, (empty[:swap], empty[:swap]), unroll=2)
 
-    def send_m(q):
+    def send_m_mirror(q):
         def to_near(o):
             def fill(k):
                 p = near(o) * cap + q * q_tiles + k
-                inverse = inverse_degree(p)
-                at = q * q_tiles + k
-                m_in[o, at, :width, :] = mean_piece(p, inverse, sums, width, width)
-                m_in[o, at, width:, :] = mean_piece(p, inverse, more, swap, swap)
+                m_in[o, q * q_tiles + k, width:, :] = mean_piece(
+                    p, inverse_degree(p), more, swap, swap
+                )
 
             each(0, q_tiles, fill)
-            m_near(q, o, me).start()
             m_near_mirror(q, o, me).start()
 
         each(1, half, to_near)
 
-    each(0, n_q, send_m)
+    each(0, n_q, send_m_mirror)
 
     def keep_m(k):
         p = me * cap + k
@@ -573,7 +586,7 @@
             features, tile_values, tile_rows, tile_cols, tile_counts, w_self, w_neigh, bias,
             part_map,
         )
-    n_y, n_m, n_q = 4, 2, 4
+    n_y, n_m, n_q = 4, 4, 4
     swap = width // 2
     wide, stay, half = width + swap, width - swap, n_bal // 2
     bf16, f32 = jnp.bfloat16, jnp.float32

time: 83.3 us -> 81.2 us (0.975); the launches traced: 82.2 us -> 81.1 us
  Pallas kernels: 80.8 us -> 79.8 us
    pallas_call x1, Pallas kernels: 80.8 us -> 79.8 us  [layer(): pl.pallas_call(functools.partial(layer_kernel, cap, slots, n_y, n_m, n_q,...]
where the time goes in v1:
time: 81.2 us; the launch traced here: 81.1 us
  Pallas kernels  79.8 us (98%)
  local copies, waits for them, and re-layouts  1.32 us (2%)
    pallas_call x1, Pallas kernels, layer(): pl.pallas_call(functools.partial(layer_kernel, cap, slots, n_y, n_m, n_q,...  79.8 us

profile of v1, /device:TPU:0, one launch (start us, length us, event | category | flops | bytes accessed | tf_op | source)
XLA Modules:
  0.0 81.1 jit_solution(10142120524743190719)
XLA Ops:
  0.0 79.8 %shard_map.91 = bf16[1,1,2048,512]{3,2,1,0:T(8,128)(2,1)S(1)} custom-call(bf16[64,8192]{1,0:T(8,128)(2,1)} %bitcast.6, bf16[128,128,128]{2,1,0:T(8,128)(2,1)} %bitcast.5, s32[4,32]{1,0:T(4,128)} %bitcast.7, s32[4,32]{1,0:T(4,128)} %bitcast.8, s32[1,4]{1,0:T(1,128)} %counts_ref.1, bf16[512,512]{1,0:T(8,128)(2,1)} %ws_hbm.1, bf16[512,512]{1,0:T(8,128)(2,1)} %wn_hbm.1, ...), custom_call_target="tpu_custom_call" | custom-call | flops 2147483648 | bytes 12582912 | tf_op jit(solution)/shard_map/pallas_call | solution.py:597
  79.8 1.3 %copy.11 = bf16[1,1,2048,512]{3,2,1,0:T(8,128)(2,1)} copy(bf16[1,1,2048,512]{3,2,1,0:T(8,128)(2,1)S(1)} %shard_map.91) | data formatting | bytes 4194304

commit v2 on v1

--- a/solution.py
+++ b/solution.py
@@ -154,7 +154,7 @@
     feat, vals_hbm, rows_ref, cols_ref, counts_ref, ws_hbm, wn_hbm, bias_ref, pm_ref,
     out_v,
     vals, own, mirror, blocks, mirrors, sums, more, f_in, f_out, f_recv, m_in, m_out, m_recv, pre,
-    ws_ref, wn_ref, table_v, table,
+    ws_ref, wn_ref, ws_t, wn_t, bias_t, table_v, table,
     vals_sem, ws_sem, wn_sem, table_sem, mir_sem,
     swap_send, swap_recv, sib_send, sib_recv, y_send, y_recv, fwd_send, fwd_recv,
     msib_send, msib_recv, my_send, my_recv, mfwd_send, mfwd_recv,
@@ -184,12 +184,12 @@
     def other(o):
         return (base + half) % n_bal + (me + o) % half
 
-    def each(first, last, body):
+    def each(first, last, body, unroll=1):
         def step(i, carry):
             body(i)
             return carry
 
-        lax.fori_loop(first, last, step, 0)
+        lax.fori_loop(first, last, step, 0, unroll=unroll)
 
     def remote(src, dst, send, recv, axis, peer):
         return pltpu.make_async_remote_copy(
@@ -218,7 +218,7 @@
         own[t] = x
         blocks[here * tiles + t] = x
 
-    each(0, tiles, pack)
+    each(0, tiles, pack, 4)
     pl.semaphore_wait(barrier, n_bal + 1)
 
     def swap_copy(i):
@@ -323,14 +323,14 @@
         def gather(k):
             f_in[o, k, :width, :] = own[table[0, near(o) * cap + k]]
 
-        each(0, cap, gather)
+        each(0, cap, gather, 4)
         f_near(o, me).start()
 
     def fill_f_other(o):
         def gather(k):
             f_out[o, k] = own[table[0, other(o) * cap + k]][:stay]
 
-        each(0, cap, gather)
+        each(0, cap, gather, 4)
 
     def keep_f(k):
         f_recv[k, own_rows, :] = own[table[0, me * cap + k]]
@@ -338,8 +338,13 @@
     each(1, half, send_f_near)
     if stay:
         each(0, half, fill_f_other)
-    each(0, cap, keep_f)
+    each(0, cap, keep_f, 4)
     load_vals.wait()
+    load_ws.wait()
+    ws_t[...] = ws_ref[...].T
+    load_wn.wait()
+    wn_t[...] = wn_ref[...].T
+    bias_t[...] = jnp.broadcast_to(bias_ref[...], (TILE, bias_ref.shape[1])).T
 
     def pass_on(i):
         y_copy(i, across).wait_recv()
@@ -364,14 +369,13 @@
         def gather(k):
             f_in[o, k, width:, :] = mirror[table[0, near(o) * cap + k]]
 
-        each(0, cap, gather)
+        each(0, cap, gather, 4)
         f_near_mirror(o, me).start()
 
     def keep_f_mirror(k):
         f_recv[k, mirror_rows, :] = mirror[table[0, me * cap + k]]
 
     each(1, half, send_f_mirror)
-    each(0, cap, keep_f_mirror)
 
     sib_copy(sibling).wait_recv()
     each(0, n_y, lambda i: fwd_copy(i, far).wait_recv())
@@ -440,7 +444,7 @@
                 p = other(o) * cap + q * q_tiles + k
                 m_out[o, q * q_tiles + k] = mean_piece(p, inverse_degree(p), sums, stay, width)
 
-            each(0, q_tiles, fill)
+            each(0, q_tiles, fill, q_tiles)
             m_other(q, o, me).start()
 
         each(0, half, to_other)
@@ -453,7 +457,7 @@
                     p, inverse_degree(p), sums, width, width
                 )
 
-            each(0, q_tiles, fill)
+            each(0, q_tiles, fill, q_tiles)
             m_near(q, o, me).start()
 
         each(1, half, to_near)
@@ -479,7 +483,7 @@
                     p, inverse_degree(p), more, swap, swap
                 )
 
-            each(0, q_tiles, fill)
+            each(0, q_tiles, fill, q_tiles)
             m_near_mirror(q, o, me).start()
 
         each(1, half, to_near)
@@ -492,9 +496,8 @@
         m_recv[k, own_rows, :] = mean_piece(p, inverse, sums, width, width)
         m_recv[k, mirror_rows, :] = mean_piece(p, inverse, more, swap, swap)
 
-    each(0, cap, keep_m)
-    load_ws.wait()
-    load_wn.wait()
+    each(0, cap, keep_m, 4)
+    each(0, cap, keep_f_mirror, 4)
 
     def wait_f_near(o):
         f_near(o, near(o)).wait_recv()
@@ -506,17 +509,12 @@
 
     rows = q_tiles * TILE
 
-    def times(recv, q, weight):
+    def times(weight, recv, q):
         x = jnp.concatenate([recv[q * q_tiles + k] for k in range(q_tiles)], axis=1)
-        return lax.dot_general(
-            x, weight[...], (((0,), (0,)), ((), ())), preferred_element_type=jnp.float32
-        )
-
-    def chunk(q):
-        return pl.ds(pl.multiple_of(q * rows, rows), rows)
+        return jnp.dot(weight[...], x, preferred_element_type=jnp.float32)
 
     def self_part(q):
-        pre[chunk(q), :] = times(f_recv, q, ws_ref) + bias_ref[...]
+        pre[q] = times(ws_t, f_recv, q) + jnp.concatenate([bias_t[...]] * q_tiles, axis=1)
 
     each(0, n_q, self_part)
     live = table[8, me * cap]
@@ -529,9 +527,10 @@
         each(1, half, wait_near)
         if stay:
             each(0, half, lambda o: m_other(q, o, other(o)).wait_recv())
-        hidden = jnp.maximum(pre[chunk(q), :] + times(m_recv, q, wn_ref), 0.0)
-        row = q * rows + lax.broadcasted_iota(jnp.int32, (rows, 1), 0)
-        out_v[0, 0, chunk(q), :] = jnp.where(row < live * TILE, hidden, 0.0).astype(jnp.bfloat16)
+        hidden = jnp.maximum(pre[q] + times(wn_t, m_recv, q), 0.0)
+        row = q * rows + lax.broadcasted_iota(jnp.int32, (1, rows), 1)
+        hidden = jnp.where(row < live * TILE, hidden, 0.0).astype(jnp.bfloat16)
+        out_v[0, 0, pl.ds(pl.multiple_of(q * rows, rows), rows), :] = hidden.T
 
     each(0, n_q, finish)
 
@@ -613,9 +612,12 @@
             pltpu.VMEM((half, cap, wide, TILE), bf16),
             pltpu.VMEM((half, cap, max(stay, 16), TILE), bf16),
             pltpu.VMEM((cap, total, TILE), bf16),
-            pltpu.VMEM((cap * TILE, total), f32),
+            pltpu.VMEM((n_q, total, cap // n_q * TILE), f32),
             pltpu.VMEM((total, total), bf16),
             pltpu.VMEM((total, total), bf16),
+            pltpu.VMEM((total, total), bf16),
+            pltpu.VMEM((total, total), bf16),
+            pltpu.VMEM((total, TILE), f32),
             pltpu.VMEM((16, TILE), jnp.int32),
             pltpu.SMEM((16, TILE), jnp.int32),
             dma, dma, dma, dma, dma,

time: 81.2 us -> 81.3 us (level)
  no operation moved by 1% of the time
where the time goes in v2:
time: 81.3 us; the launch traced here: 81.2 us
  Pallas kernels  79.9 us (98%)
  local copies, waits for them, and re-layouts  1.32 us (2%)
    pallas_call x1, Pallas kernels, layer(): pl.pallas_call(functools.partial(layer_kernel, cap, slots, n_y, n_m, n_q,...  79.9 us

profile of v2, /device:TPU:0, one launch (start us, length us, event | category | flops | bytes accessed | tf_op | source)
XLA Modules:
  0.0 81.2 jit_solution(10223491871056403978)
XLA Ops:
  0.0 79.9 %shard_map.91 = bf16[1,1,2048,512]{3,2,1,0:T(8,128)(2,1)S(1)} custom-call(bf16[64,8192]{1,0:T(8,128)(2,1)} %bitcast.6, bf16[128,128,128]{2,1,0:T(8,128)(2,1)} %bitcast.5, s32[4,32]{1,0:T(4,128)} %bitcast.7, s32[4,32]{1,0:T(4,128)} %bitcast.8, s32[1,4]{1,0:T(1,128)} %counts_ref.1, bf16[512,512]{1,0:T(8,128)(2,1)} %ws_hbm.1, bf16[512,512]{1,0:T(8,128)(2,1)} %wn_hbm.1, ...), custom_call_target="tpu_custom_call" | custom-call | flops 2147483648 | bytes 12582912 | tf_op jit(solution)/shard_map/pallas_call | solution.py:596
  79.9 1.3 %copy.11 = bf16[1,1,2048,512]{3,2,1,0:T(8,128)(2,1)} copy(bf16[1,1,2048,512]{3,2,1,0:T(8,128)(2,1)S(1)} %shard_map.91) | data formatting | bytes 4194304

commit v3 on v2

--- a/solution.py
+++ b/solution.py
@@ -151,11 +151,11 @@
 
 def layer_kernel(
     cap, slots, n_y, n_m, n_q, swap,
-    feat, vals_hbm, rows_ref, cols_ref, counts_ref, ws_hbm, wn_hbm, bias_ref, pm_ref,
+    feat_hbm, vals_hbm, rows_ref, cols_ref, counts_ref, ws_hbm, wn_hbm, bias_ref, pm_ref,
     out_v,
-    vals, own, mirror, blocks, mirrors, sums, more, f_in, f_out, f_recv, m_in, m_out, m_recv, pre,
+    feat, vals, own, mirror, blocks, mirrors, sums, more, f_in, f_out, f_recv, m_in, m_out, m_recv, pre,
     ws_ref, wn_ref, ws_t, wn_t, bias_t, table_v, table,
-    vals_sem, ws_sem, wn_sem, table_sem, mir_sem,
+    feat_sem, vals_sem, ws_sem, wn_sem, table_sem, mir_sem,
     swap_send, swap_recv, sib_send, sib_recv, y_send, y_recv, fwd_send, fwd_recv,
     msib_send, msib_recv, my_send, my_recv, mfwd_send, mfwd_recv,
     fs_sem, fr_sem, fms_sem, fmr_sem, ms_sem, mr_sem, mms_sem, mmr_sem,
@@ -167,6 +167,7 @@
     stay = width - swap
     n_bal = f_recv.shape[1] // width
     half = n_bal // 2
+    at_end = (me % half < half // 2) == (me // half == 0)
     base = me // half * half
     partner = (me + half) % n_bal
     sibling = here + 1 - 2 * (here % 2)
@@ -196,13 +197,6 @@
             src, dst, send, recv, device_id={axis: peer}, device_id_type=MESH
         )
 
-    load_vals = pltpu.make_async_copy(vals_hbm, vals, vals_sem)
-    load_vals.start()
-    load_ws = pltpu.make_async_copy(ws_hbm, ws_ref, ws_sem)
-    load_ws.start()
-    load_wn = pltpu.make_async_copy(wn_hbm, wn_ref, wn_sem)
-    load_wn.start()
-
     barrier = pltpu.get_barrier_semaphore()
     for peer in (sibling, across):
         pl.semaphore_signal(barrier, inc=1, device_id={"blk": peer}, device_id_type=MESH)
@@ -213,12 +207,27 @@
         ),
     )
 
+    span_y = y_tiles * TILE
+
+    def load_feat(i):
+        part = pl.ds(pl.multiple_of(i * span_y, span_y), span_y)
+        return pltpu.make_async_copy(feat_hbm.at[:, part], feat.at[:, part], feat_sem.at[i])
+
+    each(0, n_y, lambda i: load_feat(i).start())
+    load_vals = pltpu.make_async_copy(vals_hbm, vals, vals_sem)
+    load_ws = pltpu.make_async_copy(ws_hbm, ws_ref, ws_sem)
+    load_wn = pltpu.make_async_copy(wn_hbm, wn_ref, wn_sem)
+
     def pack(t):
         x = feat[:, pl.ds(pl.multiple_of(t * TILE, TILE), TILE)]
         own[t] = x
         blocks[here * tiles + t] = x
 
-    each(0, tiles, pack, 4)
+    def pack_part(i):
+        load_feat(i).wait()
+        each(0, y_tiles, lambda t: pack(i * y_tiles + t), 4)
+
+    each(0, n_y, pack_part)
     pl.semaphore_wait(barrier, n_bal + 1)
 
     def swap_copy(i):
@@ -314,6 +323,9 @@
     each(0, n_y, lambda i: y_copy(i, here).start())
     sib_copy(here).start()
 
+    load_vals.start()
+    load_ws.start()
+    load_wn.start()
     tables(pm_ref, rows_ref, cols_ref, counts_ref, table_v, slots, cap)
     load_table = pltpu.make_async_copy(table_v, table, table_sem)
     load_table.start()
@@ -357,8 +369,12 @@
 
     each(0, n_y, pass_on)
     each(0, n_m - 1, take_mirror)
+
+    def send_f_other():
+        each(0, half, lambda o: f_other(o, me).start())
+
     if stay:
-        each(0, half, lambda o: f_other(o, me).start())
+        pl.when(at_end)(send_f_other)
     each(n_m - 1, n_m, take_mirror)
     keep_mirror = pltpu.make_async_copy(
         mirror, mirrors.at[pl.ds(here * tiles, tiles)], mir_sem
@@ -376,6 +392,8 @@
         f_recv[k, mirror_rows, :] = mirror[table[0, me * cap + k]]
 
     each(1, half, send_f_mirror)
+    if stay:
+        pl.when(jnp.logical_not(at_end))(send_f_other)
 
     sib_copy(sibling).wait_recv()
     each(0, n_y, lambda i: fwd_copy(i, far).wait_recv())
@@ -466,10 +484,15 @@
         my_copy(i, across).wait_recv()
         mfwd_copy(i, across).start()
 
+    def send_all_m_other():
+        each(0, n_q, send_m_other)
+
     if stay:
-        each(0, n_q, send_m_other)
+        pl.when(at_end)(send_all_m_other)
     each(0, n_m, pass_mirror_on)
     each(0, n_q, send_m_near)
+    if stay:
+        pl.when(jnp.logical_not(at_end))(send_all_m_other)
     each(0, n_m, lambda i: msib_copy(i, sibling).wait_recv())
     each(0, n_m, lambda i: mfwd_copy(i, far).wait_recv())
     keep_mirror.wait()
@@ -596,9 +619,10 @@
     return pl.pallas_call(
         functools.partial(layer_kernel, cap, slots, n_y, n_m, n_q, swap),
         out_shape=pltpu.VMEM((1, 1, cap * TILE, total), bf16),
-        in_specs=[vmem, hbm, vmem, vmem, smem, hbm, hbm, vmem, vmem],
+        in_specs=[hbm, hbm, vmem, vmem, smem, hbm, hbm, vmem, vmem],
         out_specs=vmem,
         scratch_shapes=[
+            pltpu.VMEM((width, tiles * TILE), bf16),
             pltpu.VMEM((n_blk * slots, TILE, TILE), bf16),
             pltpu.VMEM((tiles, width, TILE), bf16),
             pltpu.VMEM((tiles, swap, TILE), bf16),
@@ -620,7 +644,7 @@
             pltpu.VMEM((total, TILE), f32),
             pltpu.VMEM((16, TILE), jnp.int32),
             pltpu.SMEM((16, TILE), jnp.int32),
-            dma, dma, dma, dma, dma,
+            dma((n_y,)), dma, dma, dma, dma, dma,
             dma((n_m,)), dma((n_m,)), dma, dma, dma((n_y,)), dma((n_y,)), dma((n_y,)), dma((n_y,)),
             dma((n_m,)), dma((n_m,)), dma((n_m,)), dma((n_m,)), dma((n_m,)), dma((n_m,)),
             dma((n_bal,)), dma((n_bal,)), dma((half,)), dma((n_bal,)),

time: 81.3 us -> 81.4 us (level)
  no operation moved by 1% of the time
where the time goes in v3:
time: 81.4 us; the launch traced here: 81.2 us
  Pallas kernels  79.9 us (98%)
  local copies, waits for them, and re-layouts  1.32 us (2%)
    pallas_call x1, Pallas kernels, layer(): pl.pallas_call(functools.partial(layer_kernel, cap, slots, n_y, n_m, n_q,...  79.9 us

profile of v3, /device:TPU:0, one launch (start us, length us, event | category | flops | bytes accessed | tf_op | source)
XLA Modules:
  0.0 81.2 jit_solution(1556200461505096622)
XLA Ops:
  0.0 79.9 %shard_map.91 = bf16[1,1,2048,512]{3,2,1,0:T(8,128)(2,1)S(1)} custom-call(bf16[64,8192]{1,0:T(8,128)(2,1)} %bitcast.6, bf16[128,128,128]{2,1,0:T(8,128)(2,1)} %bitcast.5, s32[4,32]{1,0:T(4,128)} %bitcast.7, s32[4,32]{1,0:T(4,128)} %bitcast.8, s32[1,4]{1,0:T(1,128)} %counts_ref.1, bf16[512,512]{1,0:T(8,128)(2,1)} %ws_hbm.1, bf16[512,512]{1,0:T(8,128)(2,1)} %wn_hbm.1, ...), custom_call_target="tpu_custom_call" | custom-call | flops 2147483648 | bytes 12582912 | tf_op jit(solution)/shard_map/pallas_call | solution.py:619
  79.9 1.3 %copy.11 = bf16[1,1,2048,512]{3,2,1,0:T(8,128)(2,1)} copy(bf16[1,1,2048,512]{3,2,1,0:T(8,128)(2,1)S(1)} %shard_map.91) | data formatting | bytes 4194304

commit v4 on v3

--- a/solution.py
+++ b/solution.py
@@ -374,27 +374,7 @@
         each(0, half, lambda o: f_other(o, me).start())
 
     if stay:
-        pl.when(at_end)(send_f_other)
-    each(n_m - 1, n_m, take_mirror)
-    keep_mirror = pltpu.make_async_copy(
-        mirror, mirrors.at[pl.ds(here * tiles, tiles)], mir_sem
-    )
-    keep_mirror.start()
-
-    def send_f_mirror(o):
-        def gather(k):
-            f_in[o, k, width:, :] = mirror[table[0, near(o) * cap + k]]
-
-        each(0, cap, gather, 4)
-        f_near_mirror(o, me).start()
-
-    def keep_f_mirror(k):
-        f_recv[k, mirror_rows, :] = mirror[table[0, me * cap + k]]
-
-    each(1, half, send_f_mirror)
-    if stay:
-        pl.when(jnp.logical_not(at_end))(send_f_other)
-
+        send_f_other()
     sib_copy(sibling).wait_recv()
     each(0, n_y, lambda i: fwd_copy(i, far).wait_recv())
 
@@ -439,6 +419,24 @@
     lax.fori_loop(
         0, HALF, absorb, (empty, empty, jnp.zeros((16, TILE), jnp.float32)), unroll=2
     )
+
+    each(n_m - 1, n_m, take_mirror)
+    keep_mirror = pltpu.make_async_copy(
+        mirror, mirrors.at[pl.ds(here * tiles, tiles)], mir_sem
+    )
+    keep_mirror.start()
+
+    def send_f_mirror(o):
+        def gather(k):
+            f_in[o, k, width:, :] = mirror[table[0, near(o) * cap + k]]
+
+        each(0, cap, gather, 4)
+        f_near_mirror(o, me).start()
+
+    def keep_f_mirror(k):
+        f_recv[k, mirror_rows, :] = mirror[table[0, me * cap + k]]
+
+    each(1, half, send_f_mirror)
 
     def inverse_degree(p):
         left, right = sums.at[table[4, p]], sums.at[table[6, p]]
@@ -609,7 +607,7 @@
             part_map,
         )
     n_y, n_m, n_q = 4, 4, 4
-    swap = width // 2
+    swap = 3 * width // 4
     wide, stay, half = width + swap, width - swap, n_bal // 2
     bf16, f32 = jnp.bfloat16, jnp.float32
     vmem = pl.BlockSpec(memory_space=pltpu.VMEM)

time: 81.4 us -> 85.1 us (1.045)
  Pallas kernels: 79.9 us -> 83.5 us
    pallas_call x1, Pallas kernels: 79.9 us -> 83.5 us  [layer(): pl.pallas_call(functools.partial(layer_kernel, cap, slots, n_y, n_m, n_q,...]
where the time goes in v4:
time: 85.1 us; the launch traced here: 84.8 us
  Pallas kernels  83.5 us (98%)
  local copies, waits for them, and re-layouts  1.32 us (2%)
    pallas_call x1, Pallas kernels, layer(): pl.pallas_call(functools.partial(layer_kernel, cap, slots, n_y, n_m, n_q,...  83.5 us

profile of v4, /device:TPU:0, one launch (start us, length us, event | category | flops | bytes accessed | tf_op | source)
XLA Modules:
  0.0 84.8 jit_solution(14851419124333675526)
XLA Ops:
  0.0 83.5 %shard_map.91 = bf16[1,1,2048,512]{3,2,1,0:T(8,128)(2,1)S(1)} custom-call(bf16[64,8192]{1,0:T(8,128)(2,1)} %bitcast.6, bf16[128,128,128]{2,1,0:T(8,128)(2,1)} %bitcast.5, s32[4,32]{1,0:T(4,128)} %bitcast.7, s32[4,32]{1,0:T(4,128)} %bitcast.8, s32[1,4]{1,0:T(1,128)} %counts_ref.1, bf16[512,512]{1,0:T(8,128)(2,1)} %ws_hbm.1, bf16[512,512]{1,0:T(8,128)(2,1)} %wn_hbm.1, ...), custom_call_target="tpu_custom_call" | custom-call | flops 2147483648 | bytes 12582912 | tf_op jit(solution)/shard_map/pallas_call | solution.py:617
  83.5 1.3 %copy.11 = bf16[1,1,2048,512]{3,2,1,0:T(8,128)(2,1)} copy(bf16[1,1,2048,512]{3,2,1,0:T(8,128)(2,1)S(1)} %shard_map.91) | data formatting | bytes 4194304

commit v5 on v3

--- a/solution.py
+++ b/solution.py
@@ -227,6 +227,9 @@
         load_feat(i).wait()
         each(0, y_tiles, lambda t: pack(i * y_tiles + t), 4)
 
+    tables(pm_ref, rows_ref, cols_ref, counts_ref, table_v, slots, cap)
+    load_table = pltpu.make_async_copy(table_v, table, table_sem)
+    load_table.start()
     each(0, n_y, pack_part)
     pl.semaphore_wait(barrier, n_bal + 1)
 
@@ -326,9 +329,6 @@
     load_vals.start()
     load_ws.start()
     load_wn.start()
-    tables(pm_ref, rows_ref, cols_ref, counts_ref, table_v, slots, cap)
-    load_table = pltpu.make_async_copy(table_v, table, table_sem)
-    load_table.start()
     load_table.wait()
 
     def send_f_near(o):

time: 81.4 us -> 81.4 us (level)
  no operation moved by 1% of the time
where the time goes in v5:
time: 81.4 us; the launch traced here: 81.2 us
  Pallas kernels  79.9 us (98%)
  local copies, waits for them, and re-layouts  1.32 us (2%)
    pallas_call x1, Pallas kernels, layer(): pl.pallas_call(functools.partial(layer_kernel, cap, slots, n_y, n_m, n_q,...  79.9 us

profile of v5, /device:TPU:0, one launch (start us, length us, event | category | flops | bytes accessed | tf_op | source)
XLA Modules:
  0.0 81.2 jit_solution(14611748361305627060)
XLA Ops:
  0.0 79.9 %shard_map.91 = bf16[1,1,2048,512]{3,2,1,0:T(8,128)(2,1)S(1)} custom-call(bf16[64,8192]{1,0:T(8,128)(2,1)} %bitcast.6, bf16[128,128,128]{2,1,0:T(8,128)(2,1)} %bitcast.5, s32[4,32]{1,0:T(4,128)} %bitcast.7, s32[4,32]{1,0:T(4,128)} %bitcast.8, s32[1,4]{1,0:T(1,128)} %counts_ref.1, bf16[512,512]{1,0:T(8,128)(2,1)} %ws_hbm.1, bf16[512,512]{1,0:T(8,128)(2,1)} %wn_hbm.1, ...), custom_call_target="tpu_custom_call" | custom-call | flops 2147483648 | bytes 12582912 | tf_op jit(solution)/shard_map/pallas_call | solution.py:619
  79.9 1.3 %copy.11 = bf16[1,1,2048,512]{3,2,1,0:T(8,128)(2,1)} copy(bf16[1,1,2048,512]{3,2,1,0:T(8,128)(2,1)S(1)} %shard_map.91) | data formatting | bytes 4194304

commit v6 on v5

--- a/solution.py
+++ b/solution.py
@@ -153,7 +153,7 @@
     cap, slots, n_y, n_m, n_q, swap,
     feat_hbm, vals_hbm, rows_ref, cols_ref, counts_ref, ws_hbm, wn_hbm, bias_ref, pm_ref,
     out_v,
-    feat, vals, own, mirror, blocks, mirrors, sums, more, f_in, f_out, f_recv, m_in, m_out, m_recv, pre,
+    feat, vals, turned, own, mirror, blocks, mirrors, sums, more, f_in, f_out, f_recv, m_in, m_out, m_recv, pre,
     ws_ref, wn_ref, ws_t, wn_t, bias_t, table_v, table,
     feat_sem, vals_sem, ws_sem, wn_sem, table_sem, mir_sem,
     swap_send, swap_recv, sib_send, sib_recv, y_send, y_recv, fwd_send, fwd_recv,
@@ -356,6 +356,12 @@
     ws_t[...] = ws_ref[...].T
     load_wn.wait()
     wn_t[...] = wn_ref[...].T
+
+    def turn(j):
+        turned[j, :TILE, :] = vals[table[1, j]].T
+        turned[j, TILE:, :] = vals[table[1, j + HALF]].T
+
+    each(0, HALF, turn, 2)
     bias_t[...] = jnp.broadcast_to(bias_ref[...], (TILE, bias_ref.shape[1])).T
 
     def pass_on(i):
@@ -405,13 +411,10 @@
 
     def products(j, held, count, extra):
         zeros = jnp.zeros((count, TILE), jnp.bfloat16)
-        a = jnp.concatenate([vals[table[1, j]], vals[table[1, j + HALF]]], axis=1)
         x = jnp.concatenate([held[table[2, j]], zeros], axis=1)
         y = jnp.concatenate([zeros, held[table[2, j + HALF]]], axis=1)
         lhs = jnp.concatenate([x, y] + extra, axis=0)
-        return lax.dot_general(
-            lhs, a, (((1,), (1,)), ((), ())), preferred_element_type=jnp.float32
-        )
+        return jnp.dot(lhs, turned[j], preferred_element_type=jnp.float32)
 
     def absorb(j, carry):
         left, right, deg = carry
@@ -624,6 +627,7 @@
         scratch_shapes=[
             pltpu.VMEM((width, tiles * TILE), bf16),
             pltpu.VMEM((n_blk * slots, TILE, TILE), bf16),
+            pltpu.VMEM((HALF, 2 * TILE, TILE), bf16),
             pltpu.VMEM((tiles, width, TILE), bf16),
             pltpu.VMEM((tiles, swap, TILE), bf16),
             pltpu.VMEM((n_blk * tiles, width, TILE), bf16),

time: 81.4 us -> 81.4 us (level)
  no operation moved by 1% of the time
where the time goes in v6:
time: 81.4 us; the launch traced here: 81.2 us
  Pallas kernels  79.9 us (98%)
  local copies, waits for them, and re-layouts  1.32 us (2%)
    pallas_call x1, Pallas kernels, layer(): pl.pallas_call(functools.partial(layer_kernel, cap, slots, n_y, n_m, n_q,...  79.9 us

profile of v6, /device:TPU:0, one launch (start us, length us, event | category | flops | bytes accessed | tf_op | source)
XLA Modules:
  0.0 81.2 jit_solution(8549541079755977945)
XLA Ops:
  0.0 79.9 %shard_map.91 = bf16[1,1,2048,512]{3,2,1,0:T(8,128)(2,1)S(1)} custom-call(bf16[64,8192]{1,0:T(8,128)(2,1)} %bitcast.6, bf16[128,128,128]{2,1,0:T(8,128)(2,1)} %bitcast.5, s32[4,32]{1,0:T(4,128)} %bitcast.7, s32[4,32]{1,0:T(4,128)} %bitcast.8, s32[1,4]{1,0:T(1,128)} %counts_ref.1, bf16[512,512]{1,0:T(8,128)(2,1)} %ws_hbm.1, bf16[512,512]{1,0:T(8,128)(2,1)} %wn_hbm.1, ...), custom_call_target="tpu_custom_call" | custom-call | flops 2147483648 | bytes 12582912 | tf_op jit(solution)/shard_map/pallas_call | solution.py:622
  79.9 1.3 %copy.11 = bf16[1,1,2048,512]{3,2,1,0:T(8,128)(2,1)} copy(bf16[1,1,2048,512]{3,2,1,0:T(8,128)(2,1)S(1)} %shard_map.91) | data formatting | bytes 4194304

commit v7 on v6

--- a/solution.py
+++ b/solution.py
@@ -611,7 +611,7 @@
             features, tile_values, tile_rows, tile_cols, tile_counts, w_self, w_neigh, bias,
             part_map,
         )
-    n_y, n_m, n_q = 4, 4, 4
+    n_y, n_m, n_q = 4, 4, 8
     swap = width // 2
     wide, stay, half = width + swap, width - swap, n_bal // 2
     bf16, f32 = jnp.bfloat16, jnp.float32

time: 81.4 us -> 82.5 us (1.014)
  Pallas kernels: 79.9 us -> 81 us
    pallas_call x1, Pallas kernels: 79.9 us -> 81 us  [layer(): pl.pallas_call(functools.partial(layer_kernel, cap, slots, n_y, n_m, n_q,...]
where the time goes in v7:
time: 82.5 us; the launch traced here: 82.3 us
  Pallas kernels  81 us (98%)
  local copies, waits for them, and re-layouts  1.32 us (2%)
    pallas_call x1, Pallas kernels, layer(): pl.pallas_call(functools.partial(layer_kernel, cap, slots, n_y, n_m, n_q,...  81 us

profile of v7, /device:TPU:0, one launch (start us, length us, event | category | flops | bytes accessed | tf_op | source)
XLA Modules:
  0.0 82.3 jit_solution(5411377691904659365)
XLA Ops:
  0.0 81.0 %shard_map.91 = bf16[1,1,2048,512]{3,2,1,0:T(8,128)(2,1)S(1)} custom-call(bf16[64,8192]{1,0:T(8,128)(2,1)} %bitcast.6, bf16[128,128,128]{2,1,0:T(8,128)(2,1)} %bitcast.5, s32[4,32]{1,0:T(4,128)} %bitcast.7, s32[4,32]{1,0:T(4,128)} %bitcast.8, s32[1,4]{1,0:T(1,128)} %counts_ref.1, bf16[512,512]{1,0:T(8,128)(2,1)} %ws_hbm.1, bf16[512,512]{1,0:T(8,128)(2,1)} %wn_hbm.1, ...), custom_call_target="tpu_custom_call" | custom-call | flops 2147483648 | bytes 12582912 | tf_op jit(solution)/shard_map/pallas_call | solution.py:622
  81.0 1.3 %copy.11 = bf16[1,1,2048,512]{3,2,1,0:T(8,128)(2,1)} copy(bf16[1,1,2048,512]{3,2,1,0:T(8,128)(2,1)S(1)} %shard_map.91) | data formatting | bytes 4194304
